TPU v7x, 512 devices: a whole 4x8x8 slice. The times are simulated.
512 devices in a mesh: aperture: 64 (over z, y_lo, x), tile: 8 (over y_hi, core).
Axes of the slice: x: 4, y: 8 (y_hi: 4, y_lo: 2; y = y_hi * 2 + y_lo), z: 8, core: 2. Of those that a mesh axis runs over, the one named last changes fastest.
Arguments:
- echoes: bfloat16 [2, 1024, 32768], P(None, 'aperture', 'tile'), may hold values from -6 to 6
- taps: bfloat16 [2, 4096], replicated, may hold values from -0.0625 to 0.0625
- steering: bfloat16 [2, 1024, 16], P(None, 'aperture'), may hold values from -1 to 1
- coefficients: float32 [2, 2, 2, 1024, 4], P(None, None, None, 'aperture'), may hold values from -2.5 to 2.5
- offsets: int32 [2, 2, 1024], P(None, None, 'aperture'), may hold values from 0 to 12
Outputs:
- image: float32 [2, 1024, 32768], P(None, 'aperture', 'tile')
Inputs may be any that keep to these rules, and one draw needn't show every extreme that they name: offsets + 3 is below 16.
All inputs are finite; a program needn't handle non-finite values.
Results may differ from a plain program's by a relative error of at most 0.0003.
Values may be sent and summed in bfloat16 or wider, within the bound.
A program may use at most 192 MiB of HBM per device.

v0:
```python
import jax
import jax.numpy as jnp
from jax import lax
from jax.experimental import pallas as pl
from jax.experimental.pallas import tpu as pltpu
from jax.sharding import PartitionSpec as P

BLOCK = 256
STEP = 512
GROUP = 1024
AHEAD = 8
HLAG = 4
EARLY = 8
EACH = 2
LAG = 4
LEVELS = 32700.0
NB = 16
BAND = 4
MESH = pl.DeviceIdType.MESH
EXACT = lax.Precision.HIGHEST
NT = (((1,), (1,)), ((), ()))


def kernel(n_tile, x_hbm, taps_hbm, steer_hbm, coef_hbm, offs_hbm, out_ref,
           data, toep, rows, acc, parts, coded, coef, offs, steer, taps,
           x_send, x_recv, f_send, f_recv, h_send, h_recv, s_send, s_recv, l_sem):
    width = data.shape[3]
    span = taps.shape[1]
    chunks = width // STEP
    blocks = STEP // BLOCK
    step_rows = blocks * 64
    groups = width // GROUP
    per = GROUP // BLOCK
    group_rows = per * 64
    lags = span // GROUP
    ratio = GROUP // STEP
    d = lax.axis_index("aperture")
    t = lax.axis_index("tile")
    x = lax.rem(d, 4)
    next_to = (d + 1 - 2 * lax.rem(x, 2), t)
    across = (d - x + 3 - x, t)
    before = (d, lax.rem(t + n_tile - 1, n_tile))
    after = (d, lax.rem(t + 1, n_tile))

    barrier = pltpu.get_barrier_semaphore()
    for other in (next_to, across):
        pl.semaphore_signal(barrier, inc=1, device_id=other, device_id_type=MESH)

    @pl.when(t < n_tile - 1)
    def _():
        pl.semaphore_signal(barrier, inc=1, device_id=after, device_id_type=MESH)

    local = [
        pltpu.make_async_copy(src, dst, l_sem.at[k])
        for k, (src, dst) in enumerate(
            [(taps_hbm, taps), (steer_hbm, steer.at[0]), (coef_hbm, coef.at[0]),
             (offs_hbm, offs.at[0]), (x_hbm, data.at[0])]
        )
    ]
    for copy in local:
        copy.start()
    pl.semaphore_wait(barrier, jnp.where(t > 0, 3, 2))

    def remote(src, dst, send, recv, where):
        return pltpu.make_async_remote_copy(
            src_ref=src, dst_ref=dst, send_sem=send, recv_sem=recv,
            device_id=where, device_id_type=MESH,
        )

    small = [
        remote(src, dst, s_send.at[k], s_recv.at[k], where)
        for k, (src, dst, where) in enumerate(
            [(coef_hbm, coef.at[1], next_to), (offs_hbm, offs.at[1], next_to),
             (steer_hbm, steer.at[1], next_to), (coef_hbm, coef.at[2], across),
             (offs_hbm, offs.at[2], across)]
        )
    ]

    def own(c):
        at = pl.ds(c * STEP, STEP)
        return remote(
            x_hbm.at[:, :, at], data.at[1, :, :, at], x_send.at[c], x_recv.at[c], next_to
        )

    def share(c):
        return remote(coded.at[0, c], coded.at[1, c], f_send.at[c], f_recv.at[c], across)

    def halo(c):
        return remote(coded.at[2, c], coded.at[3, c], h_send.at[c], h_recv.at[c], before)

    for copy in small:
        copy.start()
    for c in range(AHEAD):
        own(c).start()

    def build(part, s):
        line = taps[part : part + 1, :].astype(jnp.float32)
        padded = jnp.concatenate(
            [jnp.zeros((1, 128), jnp.float32), line, jnp.zeros((1, 256), jnp.float32)], axis=1
        )
        wide = jnp.broadcast_to(padded, (16, span + 384))
        turned = pltpu.roll(wide, s * 16, 1, stride=1, stride_axis=0).astype(jnp.bfloat16)
        toep[part, pl.ds(s * 16, 16), :] = turned[:, 128:]
        toep[part, pl.ds(128 + s * 16, 16), :] = turned[:, : span + 256]

    lane = lax.broadcasted_iota(jnp.int32, (NB, 128), 1)
    beam = lax.broadcasted_iota(jnp.int32, (NB, 128), 0)
    first = lax.rem(lane, 32) < 16
    group = lax.broadcasted_iota(jnp.int32, (32, 128), 1) // 32
    repeat = jnp.where(lax.rem(lane, 16) == beam, 1.0, 0.0)
    place0 = jnp.where(lane == beam, 1.0, 0.0).astype(jnp.bfloat16)
    place1 = jnp.where(lane == beam + 16, 1.0, 0.0).astype(jnp.bfloat16)

    def times(left, right):
        return jnp.dot(left, right, precision=EXACT, preferred_element_type=jnp.float32)

    def flipped(who, s, k):
        start = times(offs[who, s].astype(jnp.float32), repeat)
        real, imag = (times(coef[who, s, k, part], repeat) for part in range(2))
        top = jnp.zeros((NB, 128), jnp.float32)
        low = jnp.zeros((NB, 128), jnp.float32)
        for b in range(BAND):
            hit = beam.astype(jnp.float32) == start[k : k + 1] + float(b)
            re, im = real[b : b + 1], imag[b : b + 1]
            top += jnp.where(hit, jnp.where(first, re, im), 0.0)
            low += jnp.where(hit, jnp.where(first, -im, re), 0.0)
        return jnp.concatenate([top, low], axis=0)

    def view(who):
        s_re, s_im = steer[who, 0], steer[who, 1]

        def put(value, where):
            return jnp.dot(value, where, preferred_element_type=jnp.float32)

        return jnp.concatenate(
            [put(s_re, place0) + put(s_im, place1), put(s_re, place1) - put(s_im, place0)], axis=0
        )

    def columns(pair, last, views):
        once = times(views[:, :32], jnp.where(lax.rem(group, 2) == 0, *pair))
        once = jnp.concatenate(
            [jnp.where(group == 0, once[:32], 0.0), jnp.where(group == 1, once[32:], 0.0)], axis=0
        )
        return times(once, jnp.concatenate([last] * 4, axis=0))

    def weights(view0, pair, last0):
        views = jnp.concatenate([view0, view(1)], axis=0)
        mine = columns(pair, last0, views)
        theirs = columns((flipped(1, 0, 1), flipped(1, 0, 0)), flipped(2, 1, 1), views)
        side = jnp.where(jnp.concatenate([group, group], axis=0) == 0, mine, theirs)
        whole = jnp.concatenate([side, jnp.zeros_like(side)], axis=0).T[:64, :64]
        high = whole.astype(jnp.bfloat16)
        low = (whole - high.astype(jnp.float32)).astype(jnp.bfloat16)
        return jnp.concatenate([high, low], axis=0)

    eye = lax.broadcasted_iota(jnp.int32, (32, 32), 0) == lax.broadcasted_iota(
        jnp.int32, (32, 32), 1
    )
    line = lax.broadcasted_iota(jnp.int32, (16, 32), 0)
    last = 2 * STEP // 128

    def encode(slot, c, values):
        powers = jnp.zeros((16, 32), jnp.float32)
        for i, value in enumerate(values):
            peak = jnp.maximum(jnp.max(jnp.abs(value), axis=1, keepdims=True), 1e-30)
            power = jnp.ceil(16.0 * jnp.log2(peak / LEVELS))
            level = jnp.round(value * jnp.exp2(power / -16.0)).astype(jnp.int32).astype(jnp.int16)
            for k in range(2):
                for m in range(BLOCK // 128):
                    coded[slot, c, 2 * (i * BLOCK // 128 + m) + k] = level[
                        k * 16 : (k + 1) * 16, m * 128 : (m + 1) * 128
                    ]
            across_lanes = jnp.sum(jnp.where(eye, power, 0.0), axis=0, keepdims=True)
            powers = jnp.where(line == i, across_lanes, powers)
        coded[slot, c, last, :, 0:32] = powers.astype(jnp.int32).astype(jnp.int16)

    def decode(slot, c):
        powers = coded[slot, c, last, :, 0:32].astype(jnp.int32).astype(jnp.float32)
        values = []
        for i in range(blocks):
            power = jnp.sum(jnp.where(eye, powers[i : i + 1], 0.0), axis=1, keepdims=True)
            level = jnp.concatenate(
                [
                    jnp.concatenate(
                        [coded[slot, c, 2 * (i * BLOCK // 128 + m) + k] for k in range(2)], axis=0
                    )
                    for m in range(BLOCK // 128)
                ],
                axis=1,
            )
            values.append(level.astype(jnp.int32).astype(jnp.float32) * jnp.exp2(power / 16.0))
        return values

    def keep(c, values):
        for i, value in enumerate(values):
            at = c * step_rows + i * 64
            high = value.astype(jnp.bfloat16)
            rows[pl.ds(at, 32), :] = high
            rows[pl.ds(at + 32, 32), :] = (value - high.astype(jnp.float32)).astype(jnp.bfloat16)

    def cut(value):
        return [value[:, i * BLOCK : (i + 1) * BLOCK] for i in range(blocks)]

    def combine(c, matrix):
        own(c).wait_recv()
        if c + AHEAD < chunks:
            own(c + AHEAD).start()
        at = pl.ds(c * STEP, STEP)
        both = jnp.dot(
            matrix, data[:, :, :, at].reshape(64, STEP), preferred_element_type=jnp.float32
        )
        value = both[:64] + both[64:]
        encode(0, c, cut(value[32:]))
        share(c).start()
        parts[:, at] = value[:32]

    def total(c):
        share(c).wait_recv()
        mine = cut(parts[:, pl.ds(c * STEP, STEP)])
        values = [a + b for a, b in zip(mine, decode(1, c))]
        encode(2, c, values)

        @pl.when(t > 0)
        def _():
            halo(c).start()

        keep(c, values)

    def stage(q, g):
        lag = q - g
        lo, hi = (0, 0) if lag == 0 else ((lag - 1) * per + 1, lag * per)
        left = jnp.concatenate(
            [rows[pl.ds((g * per + k) * 64, group_rows), :] for k in range(lo, hi + 1)], axis=1
        )
        for part in range(2):
            term = lax.dot_general(
                left, toep[part, :, pl.ds(lo * BLOCK, (hi + 1 - lo) * BLOCK)], NT,
                preferred_element_type=jnp.float32,
            )
            if lag == 0:
                acc[part, pl.ds(g * group_rows, group_rows), :] = term
            else:
                acc[part, pl.ds(g * group_rows, group_rows), :] += term

    def finish(g):
        for i in range(per):
            at = (g * per + i) * 64
            by_re = acc[0, pl.ds(at, 32), :] + acc[0, pl.ds(at + 32, 32), :]
            by_im = acc[1, pl.ds(at, 32), :] + acc[1, pl.ds(at + 32, 32), :]
            to = pl.ds((g * per + i) * BLOCK, BLOCK)
            out_ref[0, :, to] = by_re[:NB] - by_im[NB:]
            out_ref[1, :, to] = by_re[NB:] + by_im[:NB]

    todo = [(0, build, (part, s)) for s in range(8) for part in range(2)]
    todo += [((q + 1) * ratio, stage, (q, g)) for q in range(groups) for g in range(q + 1)]
    for q in range(groups):
        todo += [((q + 1 + groups) * ratio, stage, (q + groups, g)) for g in range(q, groups)]
        todo.append(((q + 1 + groups) * ratio, finish, (q,)))

    def some(count, summed, taken):
        for _ in range(count):
            need = todo[0][0] if todo else 3 * chunks
            if need <= summed or summed == chunks and need <= chunks + taken:
                _, call, given = todo.pop(0)
                call(*given)

    def take(c):
        @pl.when(t < n_tile - 1)
        def _():
            halo(c).wait_recv()
            keep(c + chunks, decode(3, c))

        @pl.when(t == n_tile - 1)
        def _():
            rows[pl.ds((c + chunks) * step_rows, step_rows), :] = jnp.zeros(
                (step_rows, BLOCK), jnp.bfloat16
            )

    for copy in local[1:4]:
        copy.wait()
    view0, pair, last0 = view(0), (flipped(0, 0, 0), flipped(0, 0, 1)), flipped(0, 1, 0)
    local[0].wait()
    some(EARLY, 0, 0)
    local[4].wait()
    for copy in small:
        copy.wait_recv()
    matrix = weights(view0, pair, last0)
    for c in range(chunks + LAG + HLAG):
        if c < chunks:
            combine(c, matrix)
        if 0 <= c - LAG < chunks:
            total(c - LAG)
        if c >= LAG + HLAG:
            take(c - LAG - HLAG)
        some(EACH, min(c + 1 - LAG, chunks), c + 1 - LAG - HLAG)
    some(len(todo), chunks, chunks)

    for copy in small:
        copy.wait_send()
    for c in range(chunks):
        own(c).wait_send()
        share(c).wait_send()

        @pl.when(t > 0)
        def _():
            halo(c).wait_send()


def on_device(echoes, taps, steering, coefficients, offsets):
    width, span = echoes.shape[2], taps.shape[1]
    chunks = width // STEP
    blocks = (width + span) // BLOCK
    n_tile = lax.axis_size("tile")
    small = jnp.swapaxes(coefficients, 3, 4)
    dma = pltpu.SemaphoreType.DMA

    def body(*refs):
        kernel(n_tile, *refs)

    return pl.pallas_call(
        body,
        out_shape=jax.ShapeDtypeStruct((2, NB, width), jnp.float32),
        in_specs=[pl.BlockSpec(memory_space=pltpu.HBM)] * 5,
        out_specs=pl.BlockSpec(memory_space=pltpu.VMEM),
        scratch_shapes=[
            pltpu.VMEM((2, 2, NB, width), jnp.bfloat16),
            pltpu.VMEM((2, BLOCK, span + BLOCK), jnp.bfloat16),
            pltpu.VMEM((blocks * 64, BLOCK), jnp.bfloat16),
            pltpu.VMEM((2, width // BLOCK * 64, BLOCK), jnp.float32),
            pltpu.VMEM((32, width), jnp.float32),
            pltpu.VMEM((4, chunks, 2 * STEP // 128 + 1, 16, 128), jnp.int16),
            pltpu.VMEM((3,) + small.shape, jnp.float32),
            pltpu.VMEM((3,) + offsets.shape, jnp.int32),
            pltpu.VMEM((2,) + steering.shape, jnp.bfloat16),
            pltpu.VMEM(taps.shape, jnp.bfloat16),
        ]
        + [dma((chunks,))] * 6
        + [dma((5,))] * 3,
        compiler_params=pltpu.CompilerParams(
            collective_id=0, has_side_effects=True, vmem_limit_bytes=48 * 1024 * 1024
        ),
        name="backproject",
    )(
        *(
            pltpu.with_memory_space_constraint(value, pltpu.HBM)
            for value in (echoes, taps, steering, small, offsets)
        )
    )


def solution(mesh):
    in_specs = (
        P(None, "aperture", "tile"),
        P(),
        P(None, "aperture", None),
        P(None, None, None, "aperture", None),
        P(None, None, "aperture"),
    )
    out_specs = P(None, "aperture", "tile")
    return jax.shard_map(
        on_device, mesh=mesh, in_specs=in_specs, out_specs=out_specs, check_vma=False
    )
```

profile of v0, /device:TPU:1, one launch (start us, length us, event | category | flops | bytes accessed | tf_op | source)
XLA Modules:
  0.0 26.9 jit_solution(12672179243037888092)
XLA Ops:
  0.0 26.1 %backproject.1 = f32[2,16,4096]{2,1,0:T(8,128)S(1)} custom-call(bf16[2,16,4096]{2,1,0:T(8,128)(2,1)} %refs_0_.1, bf16[2,4096]{1,0:T(2,128)(2,1)} %refs_1_.1, bf16[2,16,16]{2,1,0:T(8,128)(2,1)} %refs_2_.1, f32[2,2,2,4,16]{4,3,2,1,0:T(4,128)} %bitcast.1, s32[2,2,16]{2,1,0:T(2,128)} %refs_4_.1), custom_call_target="tpu_custom_call" | custom-call | tf_op jit(solution)/shard_map/backproject/pallas_call | solution.py:320
  26.1 0.8 %copy.7 = f32[2,16,4096]{2,1,0:T(8,128)} copy(f32[2,16,4096]{2,1,0:T(8,128)S(1)} %backproject.1) | data formatting | bytes 1048576
where the time goes:
time: 27.3 us; the launch traced here: 26.9 us
  Pallas kernels  26.1 us (96%)
  local copies, waits for them, and re-layouts  0.8 us (3%)
    pallas_call x1, Pallas kernels, on_device(): pl.pallas_call(body, out_shape=jax.ShapeDtypeStruct((2, NB, width), jnp.f...  26.1 us
    unnamed x1, local copies, waits for them, and re-layouts  0.8 us

commit v1 on v0

--- a/solution.py
+++ b/solution.py
@@ -115,7 +115,10 @@
         return jnp.dot(left, right, precision=EXACT, preferred_element_type=jnp.float32)
 
     def flipped(who, s, k):
-        start = times(offs[who, s].astype(jnp.float32), repeat)
+        start = jnp.dot(
+            offs[who, s].astype(jnp.float32).astype(jnp.bfloat16), repeat.astype(jnp.bfloat16),
+            preferred_element_type=jnp.float32,
+        )
         real, imag = (times(coef[who, s, k, part], repeat) for part in range(2))
         top = jnp.zeros((NB, 128), jnp.float32)
         low = jnp.zeros((NB, 128), jnp.float32)

time: 27.3 us -> 27.2 us (level)
  no operation moved by 1% of the time
where the time goes in v1:
time: 27.2 us; the launch traced here: 26.9 us
  Pallas kernels  26.1 us (96%)
  local copies, waits for them, and re-layouts  0.8 us (3%)
    pallas_call x1, Pallas kernels, on_device(): pl.pallas_call(body, out_shape=jax.ShapeDtypeStruct((2, NB, width), jnp.f...  26.1 us
    unnamed x1, local copies, waits for them, and re-layouts  0.8 us

profile of v1, /device:TPU:1, one launch (start us, length us, event | category | flops | bytes accessed | tf_op | source)
XLA Modules:
  0.0 26.9 jit_solution(13334743020239018234)
XLA Ops:
  0.0 26.1 %backproject.1 = f32[2,16,4096]{2,1,0:T(8,128)S(1)} custom-call(bf16[2,16,4096]{2,1,0:T(8,128)(2,1)} %refs_0_.1, bf16[2,4096]{1,0:T(2,128)(2,1)} %refs_1_.1, bf16[2,16,16]{2,1,0:T(8,128)(2,1)} %refs_2_.1, f32[2,2,2,4,16]{4,3,2,1,0:T(4,128)} %bitcast.1, s32[2,2,16]{2,1,0:T(2,128)} %refs_4_.1), custom_call_target="tpu_custom_call" | custom-call | tf_op jit(solution)/shard_map/backproject/pallas_call | solution.py:323
  26.1 0.8 %copy.7 = f32[2,16,4096]{2,1,0:T(8,128)} copy(f32[2,16,4096]{2,1,0:T(8,128)S(1)} %backproject.1) | data formatting | bytes 1048576
